TPU v7x, 128 devices: a whole 4x4x4 slice. The times are simulated.
128 devices in a mesh: grp: 8 (over x_hi, y), gx: 16 (over x_lo, z, core).
Axes of the slice: x: 4 (x_hi: 2, x_lo: 2; x = x_hi * 2 + x_lo), y: 4, z: 4, core: 2. Of those that a mesh axis runs over, the one named last changes fastest.
Arguments:
- velocity: float32 [3, 128, 128, 4096], P(None, 'grp', 'gx'), may hold values from -6 to 6
- noise: float32 [3, 8, 128, 4096], P(None, None, None, 'gx'), may hold values from -6 to 6
- previous: float32 [3, 128, 4096], P(None, None, 'gx'), may hold values from -6 to 6
- decay: float32 [3, 128], replicated, may hold values from 0.6 to 0.99
- stress_factor: float32 [6, 128], replicated, may hold values from 0.2 to 1
- mean_profile: float32 [128], replicated, may hold values from 0.5 to 1.5
Outputs:
- advanced_velocity: float32 [3, 128, 128, 4096], P(None, 'grp', 'gx')
All inputs are finite; a program needn't handle non-finite values.
Results may differ from a plain program's by a relative error of at most 0.0003.
Values sent between devices are 32-bit elements; how exact they have to be, the bound alone decides.
A program may use at most 128 MiB of HBM per device.

v0:
```python
import jax
import jax.numpy as jnp
from jax import lax
from jax.sharding import PartitionSpec as P

HALF = 32


TIME_STEP = 0.15
VISCOSITY = 0.2


def with_halo(array, sides, width, wrap):
    for axis, dim in sides:
        count, length = (lax.axis_size(axis), array.shape[dim])
        up = [(i, (i + 1) % count) for i in range(count if wrap else count - 1)]
        down = [(j, i) for i, j in up]
        last = lax.slice_in_dim(array, length - width, length, axis=dim)
        leading = lax.slice_in_dim(array, 0, width, axis=dim)
        before = lax.ppermute(last, axis, up)
        after = lax.ppermute(leading, axis, down)
        array = jnp.concatenate([before, array, after], axis=dim)
    return array


def kernel_weight(offset):
    length = HALF / 2.0
    return jnp.exp(-jnp.pi * offset * offset / (2.0 * length * length))


def kernel_norm():
    offsets = jnp.arange(-HALF, HALF + 1).astype(jnp.float32)
    return jnp.sqrt(jnp.sum(kernel_weight(offsets) ** 2))


def kernel_band(rows_count, cols_count, shift):
    offsets = (jnp.arange(rows_count)[:, None] - jnp.arange(cols_count)[None, :] - shift).astype(
        jnp.float32
    )
    inside = jnp.abs(offsets) <= HALF
    return jnp.where(inside, kernel_weight(offsets) / kernel_norm(), 0.0)


def widen(noise_part):
    return with_halo(noise_part, (("gx", 3),), HALF, True)


def filter_normal(field):
    depth = field.shape[2]
    z_band = kernel_band(depth, depth, 0)
    return jnp.einsum("zw,cpwy->cpzy", z_band, field, precision=lax.Precision.HIGHEST)


def filtered(widened, span_local):
    y_band = kernel_band(span_local + 2 * HALF, span_local, HALF)
    along_y = jnp.einsum("cpzj,jy->cpzy", widened, y_band, precision=lax.Precision.HIGHEST)
    return filter_normal(along_y)


def advance(smoothed, carried, decay_col):
    scale_col = jnp.sqrt(1.0 - decay_col * decay_col)
    outputs = []
    for plane_index in range(smoothed.shape[1]):
        carried = decay_col * carried + scale_col * smoothed[:, plane_index]
        outputs.append(carried)
    return (jnp.stack(outputs, axis=1), carried)


def colour(planes, stress_factor, mean_profile):
    factor = stress_factor[:, None, :, None]
    first = mean_profile[None, :, None] + factor[0] * planes[0]
    second = factor[1] * planes[0] + factor[2] * planes[1]
    third = factor[3] * planes[0] + factor[4] * planes[1] + factor[5] * planes[2]
    return jnp.stack([first, second, third])


def to_owners(generated):
    return lax.all_to_all(generated, "gx", split_axis=2, concat_axis=3, tiled=True)


def tendency(padded):
    centre = padded[:, 1:-1, 1:-1]
    x_next = padded[:, 2:, 1:-1]
    x_prev = padded[:, :-2, 1:-1]
    z_next = padded[:, 1:-1, 2:]
    z_prev = padded[:, 1:-1, :-2]
    y_next = jnp.roll(centre, -1, axis=3)
    y_prev = jnp.roll(centre, 1, axis=3)
    advect = centre[0:1] * (x_next - x_prev) * 0.5
    advect = advect + centre[1:2] * (z_next - z_prev) * 0.5
    advect = advect + centre[2:3] * (y_next - y_prev) * 0.5
    spread = x_next + x_prev + z_next + z_prev + y_next + y_prev - 6.0 * centre
    return -advect + VISCOSITY * spread


def faces(field):
    return with_halo(field, (("grp", 1), ("gx", 2)), 1, False)


def local(velocity, noise, previous, decay, stress_factor, mean_profile):
    row_index = lax.axis_index("grp")
    span_local = noise.shape[3]
    plane_count = noise.shape[1]
    decay_col = decay[:, :, None]
    widened = widen(noise)

    def produce():
        smoothed = filtered(widened, span_local)
        planes, unused = advance(smoothed, previous, decay_col)
        return colour(planes, stress_factor, mean_profile)

    def nothing():
        return jnp.zeros(noise.shape, jnp.float32)

    generated = lax.cond(row_index == 0, produce, nothing)
    slab_planes = to_owners(generated)
    updated = jnp.concatenate([slab_planes, velocity[:, plane_count:]], axis=1)
    start = jnp.where(row_index == 0, updated, velocity)
    section = start + TIME_STEP * tendency(faces(start))
    second = section + TIME_STEP * tendency(faces(section))
    return 0.5 * start + 0.5 * second


def solution(mesh):
    placed = (
        P(None, "grp", "gx", None),
        P(None, None, None, "gx"),
        P(None, None, "gx"),
        P(),
        P(),
        P(),
    )
    return jax.shard_map(
        local, mesh=mesh, in_specs=placed, out_specs=P(None, "grp", "gx", None), check_vma=False
    )
```

profile of v0, /device:TPU:2, one launch (start us, length us, event | category | flops | bytes accessed | tf_op | source)
XLA Modules:
  0.0 207.1 jit_solution(12641527653824072600)
XLA Ops:
  0.0 2.4 %copy.52 = f32[3,8,128,256]{2,3,1,0:T(8,128)S(1)} copy(f32[3,8,128,256]{3,2,1,0:T(8,128)} %param.9) | data formatting | bytes 6291456 | tf_op args[1]
  2.4 0.0 copy-start.3
  2.4 0.8 fusion.79
  3.2 3.9 %collective-permute-start.1 = (f32[3,8,128,32]{2,3,1,0:T(8,128)S(1)}, f32[3,8,128,32]{2,3,1,0:T(8,128)}, u32[]{:S(2)}, u32[]{:S(2)}) collective-permute-start(f32[3,8,128,32]{2,3,1,0:T(8,128)S(1)} %get-tuple-element.90), channel_id=1, source_target_pairs={{1,0},{2,1},{3,2},{4,3},{5,4},{6,5},{7,6},{8,7},{9,8},{10,9},{11,1... | collective-permute-start | bytes 1179656 | tf_op jit(solution)/shard_map/ppermute | solution.py:21
  7.1 5.8 %collective-permute-done = f32[3,8,128,32]{2,3,1,0:T(8,128)} collective-permute-done((f32[3,8,128,32]{2,3,1,0:T(8,128)}, f32[3,8,128,32]{2,3,1,0:T(8,128)}, u32[]{:S(2)}, u32[]{:S(2)}) %collective-permute-start) | collective-permute-done | bytes 393248 | tf_op jit(solution)/shard_map/ppermute | solution.py:20
  12.8 3.4 %pad_maximum_fusion.21 = f32[3,8,128,320]{2,3,1,0:T(8,128)} fusion(f32[3,8,128,32]{2,3,1,0:T(8,128)} %collective-permute-done.1, f32[3,8,128,256]{2,3,1,0:T(8,128)S(1)} %copy.52, f32[3,8,128,32]{2,3,1,0:T(8,128)} %collective-permute-done), kind=kLoop, calls=%fused_computation.120 | loop fusion | flops 1966080 | bytes 7864320 | tf_op jit(solution)/shard_map/concatenate | solution.py:22
  16.3 15.0 %conditional.1 = (f32[3,8,128,256]{2,3,0,1:T(8,128)S(1)}) conditional(s32[]{:T(128)} %convert_element_type.17, () %tuple.11, (f32[128]{0:T(128)}, f32[6,128]{1,0:T(8,128)S(1)}, f32[3,128]{1,0:T(4,128)S(1)}, f32[3,128,256]{2,1,0:T(8,128)}, f32[3,8,128,320]{2,3,1,0:T(8,128)}) %tuple.43), branch_computations={%region_0.0_spmd, %region_1.3_spmd} | conditional | flops 4236559616 | bytes 38985412 | solution.py:115
  16.3 0.6 fusion.60
  17.6 7.7 %fusion.29 = f32[256,3,8,128]{3,0,2,1:T(8,128)S(1)} fusion(f32[3,8,128,320]{2,3,1,0:T(8,128)} %get-tuple-element.23, f32[]{:T(128)S(6)} %sqrt.7), kind=kOutput, calls=%fused_computation.47 | convolution fusion | flops 3020718080 | bytes 7077892 | tf_op jit(solution)/shard_map/cond/branch_1_fun/cpzj,jy->cpzy/dot_general | solution.py:56
  25.3 2.6 %fusion.2 = f32[3,8,128,256]{2,3,1,0:T(8,128)S(1)} fusion(f32[256,3,8,128]{3,0,2,1:T(8,128)S(1)} %fusion.29, f32[]{:T(128)S(6)} %sqrt.7), kind=kOutput, calls=%fused_computation.3 | convolution fusion | flops 1208107008 | bytes 6291460 | tf_op jit(solution)/shard_map/cond/branch_1_fun/zw,cpwy->cpzy/dot_general | solution.py:51
  27.9 0.6 slice_bitcast_fusion.13
  28.5 1.2 copy.55
  29.7 0.0 copy-start.9
  29.8 0.1 bitcast_dynamic-update-slice_fusion.5
  30.0 0.1 bitcast_dynamic-update-slice_fusion.3
  30.1 0.1 bitcast_dynamic-update-slice_fusion.1
  30.3 0.1 fusion.9
  30.4 0.5 multiply_add_fusion.1
  30.9 0.2 pad_maximum_fusion
  31.3 2.4 %copy.56 = f32[3,8,128,256]{3,1,0,2:T(8,128)} copy(f32[3,8,128,256]{2,3,0,1:T(8,128)S(1)} %get-tuple-element.91) | data formatting | bytes 6291456 | tf_op jit(solution)/shard_map/cond | solution.py:115
  33.6 6.0 %all-to-all-start = ((f32[3,8,128,256]{3,1,0,2:T(8,128)}), f32[3,8,128,256]{3,1,0,2:T(8,128)S(1)}, u32[]{:S(2)}, u32[]{:S(2)}) async-start(f32[3,8,128,256]{3,1,0,2:T(8,128)} %copy.56), calls=%async_computation | async-start | bytes 6291456 | tf_op jit(solution)/shard_map/all_to_all | solution.py:78
  39.7 3.9 %slice.173 = f32[3,8,8,4096]{3,2,1,0:T(8,128)} slice(f32[3,16,8,4096]{3,2,1,0:T(8,128)} %param.8), slice={[0:3], [8:16], [0:8], [0:4096]} | slice | bytes 6291456 | tf_op jit(solution)/shard_map/slice | solution.py:117
  43.5 35.5 %all-to-all-done = f32[3,8,128,256]{3,1,0,2:T(8,128)S(1)} async-done(((f32[3,8,128,256]{3,1,0,2:T(8,128)}), f32[3,8,128,256]{3,1,0,2:T(8,128)S(1)}, u32[]{:S(2)}, u32[]{:S(2)}) %all-to-all-start) | async-done | bytes 3145760 | tf_op jit(solution)/shard_map/all_to_all | solution.py:78
  79.0 1.0 copy.57
  80.0 0.9 copy-done.1
  80.9 1.0 maximum_select_fusion
  81.9 0.9 fusion.76
  82.8 1.3 collective-permute-start.3
  84.1 1.3 collective-permute-start.2
  85.4 7.2 %fusion.77 = (f32[3,16,8,4095]{3,2,1,0:T(8,128)}, f32[3,16,8,4095]{3,2,1,0:T(8,128)}) fusion(f32[3,16,8,4096]{3,2,1,0:T(8,128)S(1)} %maximum_select_fusion), kind=kLoop, calls=%fused_computation.137 | loop fusion | bytes 25159680 | tf_op jit(solution)/shard_map/jit(_roll_static)/slice | solution.py:87
  92.6 0.1 fusion.78
  92.7 0.1 collective-permute-done.3
  92.8 4.1 %collective-permute-done.2 = f32[3,1,8,4096]{3,2,1,0:T(8,128)} collective-permute-done((f32[3,1,8,4096]{3,2,1,0:T(8,128)}, f32[3,1,8,4096]{3,2,1,0:T(8,128)}, u32[]{:S(2)}, u32[]{:S(2)}) %collective-permute-start.2) | collective-permute-done | bytes 393248 | tf_op jit(solution)/shard_map/ppermute | solution.py:21
  97.0 2.7 %pad_maximum_fusion.25 = (f32[3,18,1,4096]{3,2,1,0:T(1,128)S(1)}, f32[3,18,1,4096]{3,2,1,0:T(1,128)S(1)}) fusion(f32[3,1,8,4096]{3,2,1,0:T(8,128)} %collective-permute-done.2, f32[3,16,8,4096]{3,2,1,0:T(8,128)S(1)} %maximum_select_fusion, f32[3,1,8,4096]{3,2,1,0:T(8,128)S(1)} %collective-permute-done.3), kind=kLoop, calls=%fused_computation.130 | loop fusion | flops 884736 | bytes 8847360 | tf_op jit(solution)/shard_map/concatenate | solution.py:22
  99.6 0.5 copy.60
  100.2 0.0 slice-start.4
  100.2 0.5 copy.58
  100.7 0.0 slice-start.5
  100.7 10.6 %collective-permute-start.4 = (f32[3,18,1,4096]{3,1,2,0:T(8,128)S(1)}, f32[3,18,1,4096]{3,1,2,0:T(8,128)S(1)}, u32[]{:S(2)}, u32[]{:S(2)}) collective-permute-start(f32[3,18,1,4096]{3,1,2,0:T(8,128)S(1)} %copy.58), channel_id=1, source_target_pairs={{1,0},{2,1},{3,2},{4,3},{5,4},{6,5},{7,6},{8,7},{9,8},{10,9},{11,1... | collective-permute-start | bytes 2654216 | tf_op jit(solution)/shard_map/ppermute | solution.py:21
  111.3 1.9 collective-permute-start.5
  113.3 2.0 slice_bitcast_fusion.19
  115.3 9.8 %collective-permute-done.4 = f32[3,18,1,4096]{3,1,2,0:T(8,128)S(1)} collective-permute-done((f32[3,18,1,4096]{3,1,2,0:T(8,128)S(1)}, f32[3,18,1,4096]{3,1,2,0:T(8,128)S(1)}, u32[]{:S(2)}, u32[]{:S(2)}) %collective-permute-start.4) | collective-permute-done | bytes 884768 | tf_op jit(solution)/shard_map/ppermute | solution.py:21
  125.0 1.9 copy.59
  126.9 4.0 %collective-permute-done.5 = f32[3,18,1,4096]{3,1,2,0:T(8,128)S(1)} collective-permute-done((f32[3,18,1,4096]{3,1,2,0:T(8,128)S(1)}, f32[3,18,1,4096]{3,1,2,0:T(8,128)S(1)}, u32[]{:S(2)}, u32[]{:S(2)}) %collective-permute-start.5) | collective-permute-done | bytes 884768 | tf_op jit(solution)/shard_map/ppermute | solution.py:20
  131.0 1.9 copy.61
  132.9 11.3 %multiply_add_fusion.2 = f32[3,16,8,4096]{3,2,1,0:T(8,128)S(1)} fusion(f32[3,16,8,4096]{3,2,1,0:T(8,128)S(1)} %maximum_select_fusion, f32[3,16,8,4095]{3,2,1,0:T(8,128)} %get-tuple-element.86, f32[3,16,8,1]{3,2,1,0:T(8,128)S(1)} %get-tuple-element.88, f32[3,16,8,1]{3,2,1,0:T(8,128)S(1)} %get-tuple-element.87, f32[3,16,8,4095]{3,2,1,0:T(8,128)S(1)} %bitcast.158, ...), kind=kLoop, calls=%fused_computation.119 | loop fusion | flops 48758784 | bytes 34013184 | tf_op jit(solution)/shard_map/add | solution.py:119
  144.2 2.7 %copy-done = f32[3,16,8,4096]{3,2,1,0:T(8,128)} copy-done((f32[3,16,8,4096]{3,2,1,0:T(8,128)}, f32[3,16,8,4096]{3,2,1,0:T(8,128)S(1)}, u32[]{:S(2)}) %copy-start) | copy-done | bytes 6291480
  146.9 0.9 fusion.73
  147.8 1.5 collective-permute-start.7
  149.3 1.5 collective-permute-start.6
  150.8 11.0 %fusion.74 = (f32[3,16,8,4095]{3,2,1,0:T(8,128)}, f32[3,16,8,4095]{3,2,1,0:T(8,128)}) fusion(f32[3,16,8,4096]{3,2,1,0:T(8,128)} %copy-done), kind=kLoop, calls=%fused_computation.134 | loop fusion | bytes 25159680 | tf_op jit(solution)/shard_map/jit(_roll_static)/slice | solution.py:87
  161.8 1.3 fusion.75
  163.1 0.0 slice-start.1
  163.2 6.0 %pad_maximum_fusion.22 = (f32[3,18,1,4096]{3,2,1,0:T(1,128)S(1)}, f32[3,18,1,4096]{3,2,1,0:T(1,128)S(1)}) fusion(f32[3,1,8,4096]{3,2,1,0:T(8,128)} %collective-permute-done.6, f32[3,16,8,4096]{3,2,1,0:T(8,128)} %copy-done, f32[3,1,8,4096]{3,2,1,0:T(8,128)S(1)} %collective-permute-done.7), kind=kLoop, calls=%fused_computation.127 | loop fusion | flops 884736 | bytes 8847360 | tf_op jit(solution)/shard_map/concatenate | solution.py:22
  169.1 0.5 copy.64
  169.7 0.5 copy.62
  170.2 2.2 %collective-permute-start.8 = (f32[3,18,1,4096]{3,1,2,0:T(8,128)S(1)}, f32[3,18,1,4096]{3,1,2,0:T(8,128)S(1)}, u32[]{:S(2)}, u32[]{:S(2)}) collective-permute-start(f32[3,18,1,4096]{3,1,2,0:T(8,128)S(1)} %copy.62), channel_id=1, source_target_pairs={{1,0},{2,1},{3,2},{4,3},{5,4},{6,5},{7,6},{8,7},{9,8},{10,9},{11,1... | collective-permute-start | bytes 2654216 | tf_op jit(solution)/shard_map/ppermute | solution.py:21
  172.4 2.4 %collective-permute-start.9 = (f32[3,18,1,4096]{3,1,2,0:T(8,128)S(1)}, f32[3,18,1,4096]{3,1,2,0:T(8,128)S(1)}, u32[]{:S(2)}, u32[]{:S(2)}) collective-permute-start(f32[3,18,1,4096]{3,1,2,0:T(8,128)S(1)} %copy.64), channel_id=1, source_target_pairs={{0,1},{1,2},{2,3},{3,4},{4,5},{5,6},{6,7},{7,8},{8,9},{9,10},{10,1... | collective-permute-start | bytes 2654216 | tf_op jit(solution)/shard_map/ppermute | solution.py:20
  174.9 2.8 %slice_bitcast_fusion.16 = (f32[16,8,4096]{2,1,0:T(8,128)}, f32[16,8,4096]{2,1,0:T(8,128)}, f32[16,8,4096]{2,1,0:T(8,128)}) fusion(f32[3,16,8,4096]{3,2,1,0:T(8,128)S(1)} %bitcast.154), kind=kLoop, calls=%fused_computation.123 | loop fusion | bytes 12582912 | tf_op jit(solution)/shard_map/mul | solution.py:89
  177.7 8.4 %collective-permute-done.8 = f32[3,18,1,4096]{3,1,2,0:T(8,128)S(1)} collective-permute-done((f32[3,18,1,4096]{3,1,2,0:T(8,128)S(1)}, f32[3,18,1,4096]{3,1,2,0:T(8,128)S(1)}, u32[]{:S(2)}, u32[]{:S(2)}) %collective-permute-start.8) | collective-permute-done | bytes 884768 | tf_op jit(solution)/shard_map/ppermute | solution.py:21
  186.1 0.9 copy.63
  187.0 5.0 %collective-permute-done.9 = f32[3,18,1,4096]{3,1,2,0:T(8,128)S(1)} collective-permute-done((f32[3,18,1,4096]{3,1,2,0:T(8,128)S(1)}, f32[3,18,1,4096]{3,1,2,0:T(8,128)S(1)}, u32[]{:S(2)}, u32[]{:S(2)}) %collective-permute-start.9) | collective-permute-done | bytes 884768 | tf_op jit(solution)/shard_map/ppermute | solution.py:20
  192.0 1.9 copy.65
  193.9 12.9 %add_multiply_fusion = f32[3,16,8,4096]{3,2,1,0:T(8,128)} fusion(f32[3,16,8,4096]{3,2,1,0:T(8,128)S(1)} %maximum_select_fusion, f32[3,16,8,4096]{3,2,1,0:T(8,128)S(1)} %bitcast.154, f32[3,16,8,4095]{3,2,1,0:T(8,128)} %get-tuple-element.77, f32[3,16,8,1]{3,2,1,0:T(8,128)S(1)} %get-tuple-element.79, f32[3,16,8,1]{3,2,1,0:T(8,128)S(1)} %get-tuple-element.78, ...), kind=kLoop, calls=%fused_computation.118 | loop fusion | flops 51904512 | bytes 40304640 | tf_op jit(solution)/shard_map/add | solution.py:121
  (37 shorter events, 0.3 us)
Async XLA Ops:
  2.4 13.9 %copy-start.2 = (f32[3,128]{1,0:T(4,128)S(1)}, f32[3,128]{1,0:T(4,128)}, u32[]{:S(2)}) copy-start(f32[3,128]{1,0:T(4,128)} %param.11) | copy-start | bytes 4612
  2.4 13.9 %copy-start.3 = (f32[6,128]{1,0:T(8,128)S(1)}, f32[6,128]{1,0:T(8,128)}, u32[]{:S(2)}) copy-start(f32[6,128]{1,0:T(8,128)} %param.12) | copy-start | bytes 9220
  3.2 9.6 %collective-permute-start = (f32[3,8,128,32]{2,3,1,0:T(8,128)}, f32[3,8,128,32]{2,3,1,0:T(8,128)}, u32[]{:S(2)}, u32[]{:S(2)}) collective-permute-start(f32[3,8,128,32]{2,3,1,0:T(8,128)} %get-tuple-element.89), channel_id=1, source_target_pairs={{0,1},{1,2},{2,3},{3,4},{4,5},{5,6},{6,7},{7,8},{8,9},{9,10},{10,1... | collective-permute-start | bytes 1179656 | tf_op jit(solution)/shard_map/ppermute | solution.py:20
  3.2 9.6 %collective-permute-start.1 = (f32[3,8,128,32]{2,3,1,0:T(8,128)S(1)}, f32[3,8,128,32]{2,3,1,0:T(8,128)}, u32[]{:S(2)}, u32[]{:S(2)}) collective-permute-start(f32[3,8,128,32]{2,3,1,0:T(8,128)S(1)} %get-tuple-element.90), channel_id=1, source_target_pairs={{1,0},{2,1},{3,2},{4,3},{5,4},{6,5},{7,6},{8,7},{9,8},{10,9},{11,1... | collective-permute-start | bytes 1179656 | tf_op jit(solution)/shard_map/ppermute | solution.py:21
  29.7 0.7 copy-start.4
  29.7 0.7 copy-start.5
  29.7 0.7 copy-start.6
  29.7 0.7 copy-start.7
  29.7 0.7 copy-start.8
  29.7 0.7 copy-start.9
  33.6 45.3 %all-to-all-start = ((f32[3,8,128,256]{3,1,0,2:T(8,128)}), f32[3,8,128,256]{3,1,0,2:T(8,128)S(1)}, u32[]{:S(2)}, u32[]{:S(2)}) async-start(f32[3,8,128,256]{3,1,0,2:T(8,128)} %copy.56), calls=%async_computation | async-start | bytes 6291456 | tf_op jit(solution)/shard_map/all_to_all | solution.py:78
  79.0 1.9 copy-start.1
  82.8 10.0 %collective-permute-start.3 = (f32[3,1,8,4096]{3,2,1,0:T(8,128)}, f32[3,1,8,4096]{3,2,1,0:T(8,128)S(1)}, u32[]{:S(2)}, u32[]{:S(2)}) collective-permute-start(f32[3,1,8,4096]{3,2,1,0:T(8,128)} %get-tuple-element.83), channel_id=1, source_target_pairs={{0,16},{16,32},{32,48},{48,64},{64,80},{80,96},{96,112},{1,17},{17... | collective-permute-start | bytes 1179656 | tf_op jit(solution)/shard_map/ppermute | solution.py:20
  84.1 12.9 %collective-permute-start.2 = (f32[3,1,8,4096]{3,2,1,0:T(8,128)}, f32[3,1,8,4096]{3,2,1,0:T(8,128)}, u32[]{:S(2)}, u32[]{:S(2)}) collective-permute-start(f32[3,1,8,4096]{3,2,1,0:T(8,128)} %get-tuple-element.84), channel_id=1, source_target_pairs={{16,0},{32,16},{48,32},{64,48},{80,64},{96,80},{112,96},{17,1},{33... | collective-permute-start | bytes 1179656 | tf_op jit(solution)/shard_map/ppermute | solution.py:21
  100.2 32.7 %slice-start.4 = ((s8[6291456]{0:T(1024)(128)(4,1)}), s8[4194304]{0:T(1024)(128)(4,1)S(1)}, s32[]{:S(2)}) async-start(s8[6291456]{0:T(1024)(128)(4,1)} %bitcast.157), calls=%async_computation.5 | async-start | bytes 8388608
  100.7 32.2 %slice-start.5 = ((s8[6291456]{0:T(1024)(128)(4,1)}), s8[2097152]{0:T(1024)(128)(4,1)S(1)}, s32[]{:S(2)}) async-start(s8[6291456]{0:T(1024)(128)(4,1)} %bitcast.157), calls=%async_computation.6 | async-start | bytes 4194304
  100.7 24.3 %collective-permute-start.4 = (f32[3,18,1,4096]{3,1,2,0:T(8,128)S(1)}, f32[3,18,1,4096]{3,1,2,0:T(8,128)S(1)}, u32[]{:S(2)}, u32[]{:S(2)}) collective-permute-start(f32[3,18,1,4096]{3,1,2,0:T(8,128)S(1)} %copy.58), channel_id=1, source_target_pairs={{1,0},{2,1},{3,2},{4,3},{5,4},{6,5},{7,6},{8,7},{9,8},{10,9},{11,1... | collective-permute-start | bytes 2654216 | tf_op jit(solution)/shard_map/ppermute | solution.py:21
  111.3 19.6 %collective-permute-start.5 = (f32[3,18,1,4096]{3,1,2,0:T(8,128)S(1)}, f32[3,18,1,4096]{3,1,2,0:T(8,128)S(1)}, u32[]{:S(2)}, u32[]{:S(2)}) collective-permute-start(f32[3,18,1,4096]{3,1,2,0:T(8,128)S(1)} %copy.60), channel_id=1, source_target_pairs={{0,1},{1,2},{2,3},{3,4},{4,5},{5,6},{6,7},{7,8},{8,9},{9,10},{10,1... | collective-permute-start | bytes 2654216 | tf_op jit(solution)/shard_map/ppermute | solution.py:20
  144.2 2.7 %copy-start = (f32[3,16,8,4096]{3,2,1,0:T(8,128)}, f32[3,16,8,4096]{3,2,1,0:T(8,128)S(1)}, u32[]{:S(2)}) copy-start(f32[3,16,8,4096]{3,2,1,0:T(8,128)S(1)} %multiply_add_fusion.2) | copy-start | bytes 18874372
  147.8 15.3 %collective-permute-start.7 = (f32[3,1,8,4096]{3,2,1,0:T(8,128)}, f32[3,1,8,4096]{3,2,1,0:T(8,128)S(1)}, u32[]{:S(2)}, u32[]{:S(2)}) collective-permute-start(f32[3,1,8,4096]{3,2,1,0:T(8,128)} %get-tuple-element.74), channel_id=1, source_target_pairs={{0,16},{16,32},{32,48},{48,64},{64,80},{80,96},{96,112},{1,17},{17... | collective-permute-start | bytes 1179656 | tf_op jit(solution)/shard_map/ppermute | solution.py:20
  149.3 13.8 %collective-permute-start.6 = (f32[3,1,8,4096]{3,2,1,0:T(8,128)}, f32[3,1,8,4096]{3,2,1,0:T(8,128)}, u32[]{:S(2)}, u32[]{:S(2)}) collective-permute-start(f32[3,1,8,4096]{3,2,1,0:T(8,128)} %get-tuple-element.75), channel_id=1, source_target_pairs={{16,0},{32,16},{48,32},{64,48},{80,64},{96,80},{112,96},{17,1},{33... | collective-permute-start | bytes 1179656 | tf_op jit(solution)/shard_map/ppermute | solution.py:21
  161.8 13.0 %slice-start = ((s8[6291456]{0:T(1024)(128)(4,1)}), s8[4194304]{0:T(1024)(128)(4,1)S(1)}, s32[]{:S(2)}) async-start(s8[6291456]{0:T(1024)(128)(4,1)} %bitcast.153), calls=%async_computation.1 | async-start | bytes 8388608
  163.1 11.7 %slice-start.1 = ((s8[6291456]{0:T(1024)(128)(4,1)}), s8[2097152]{0:T(1024)(128)(4,1)S(1)}, s32[]{:S(2)}) async-start(s8[6291456]{0:T(1024)(128)(4,1)} %bitcast.153), calls=%async_computation.2 | async-start | bytes 4194304
  169.7 24.3 %slice-start.2 = ((s8[6291456]{0:T(1024)(128)(4,1)}), s8[4194304]{0:T(1024)(128)(4,1)S(1)}, s32[]{:S(2)}) async-start(s8[6291456]{0:T(1024)(128)(4,1)} %bitcast.155), calls=%async_computation.3 | async-start | bytes 8388608
  170.2 23.7 %slice-start.3 = ((s8[6291456]{0:T(1024)(128)(4,1)}), s8[2097152]{0:T(1024)(128)(4,1)S(1)}, s32[]{:S(2)}) async-start(s8[6291456]{0:T(1024)(128)(4,1)} %bitcast.155), calls=%async_computation.4 | async-start | bytes 4194304
  170.2 15.9 %collective-permute-start.8 = (f32[3,18,1,4096]{3,1,2,0:T(8,128)S(1)}, f32[3,18,1,4096]{3,1,2,0:T(8,128)S(1)}, u32[]{:S(2)}, u32[]{:S(2)}) collective-permute-start(f32[3,18,1,4096]{3,1,2,0:T(8,128)S(1)} %copy.62), channel_id=1, source_target_pairs={{1,0},{2,1},{3,2},{4,3},{5,4},{6,5},{7,6},{8,7},{9,8},{10,9},{11,1... | collective-permute-start | bytes 2654216 | tf_op jit(solution)/shard_map/ppermute | solution.py:21
  172.4 19.6 %collective-permute-start.9 = (f32[3,18,1,4096]{3,1,2,0:T(8,128)S(1)}, f32[3,18,1,4096]{3,1,2,0:T(8,128)S(1)}, u32[]{:S(2)}, u32[]{:S(2)}) collective-permute-start(f32[3,18,1,4096]{3,1,2,0:T(8,128)S(1)} %copy.64), channel_id=1, source_target_pairs={{0,1},{1,2},{2,3},{3,4},{4,5},{5,6},{6,7},{7,8},{8,9},{9,10},{10,1... | collective-permute-start | bytes 2654216 | tf_op jit(solution)/shard_map/ppermute | solution.py:20
where the time goes:
time: 209 us; the launch traced here: 207 us
  waiting for transfers between devices  72.7 us (35%)
  local copies, waits for them, and re-layouts  50.9 us (24%)
  other arithmetic  39.1 us (19%)
  starting transfers between devices  32.6 us (16%)
  matrix products  10.3 us (5%)
    all_to_all x1, waiting for transfers between devices, to_owners(): lax.all_to_all(generated, 'gx', split_axis=2, concat_axis=3, tiled=True)  35.5 us
    ppermute x5, waiting for transfers between devices, with_halo(): after = lax.ppermute(leading, axis, down)  22.3 us
    slice x4, local copies, waits for them, and re-layouts, tendency(): y_next = jnp.roll(centre, -1, axis=3)  19.6 us
    ppermute x5, starting transfers between devices, with_halo(): after = lax.ppermute(leading, axis, down)  19.4 us
    ppermute x5, waiting for transfers between devices, with_halo(): before = lax.ppermute(last, axis, up)  14.9 us
    add x1, other arithmetic, local(): return 0.5 * start + 0.5 * second  12.9 us
    concatenate x3, other arithmetic, with_halo(): array = jnp.concatenate([before, array, after], axis=dim)  12 us
    add x1, other arithmetic, local(): section = start + TIME_STEP * tendency(faces(start))  11.3 us
  transfers between devices with their start and end apart: 11, of which 8 were waited for; matrix products, arithmetic and copies ran while one was open for 15% of the time, Pallas kernels for 0%

commit v1 on v0

v1 whole, which is shorter than its diff:
```python
import functools

import jax
import jax.numpy as jnp
import ml_dtypes
import numpy as np
from jax import lax
from jax.experimental import pallas as pl
from jax.experimental.pallas import tpu as pltpu
from jax.sharding import PartitionSpec as P

HALF = 32
TIME_STEP = 0.15
VISCOSITY = 0.2
PL = 8
ROWS, COLS = 8, 16
NX, NZ, NY = 16, 8, 4096
SPAN = NY // COLS
DEPTH = NZ * COLS
WIDE = 512
MESH = pl.DeviceIdType.MESH
F32, BF16 = jnp.float32, jnp.bfloat16

PLANES = {0: (0, 4, 5, 6), 1: (1,), 3: (2,), 4: (3, 7)}
SLOTS = max(len(v) for v in PLANES.values())
OWNER = {p: (r, j) for r, v in PLANES.items() for j, p in enumerate(v)}

GROUPS = ((0, 2), (2, 2), (4, 2), (6, 2), (8, 4), (12, 4))
NG = len(GROUPS)


def weights():
    k = np.arange(-HALF, HALF + 1, dtype=np.float64)
    length = HALF / 2.0
    w = np.exp(-np.pi * k * k / (2.0 * length * length))
    w = w / np.sqrt(np.sum(w * w))

    def band(distance):
        inside = np.abs(distance) <= HALF
        return np.where(inside, w[np.clip(distance + HALF, 0, 2 * HALF)], 0.0)

    cols = np.arange(SPAN)[None, :]
    main = band(np.arange(SPAN)[:, None] - cols)
    wy = np.zeros((3, SPAN + 256, SPAN))
    for c in range(3):
        wy[c, :SPAN] = main
        rim = np.arange(HALF)[:, None]
        wy[c, SPAN + HALF * c : SPAN + HALF * (c + 1)] = band(rim - HALF - cols)
        wy[c, SPAN + 128 + HALF * c : SPAN + 128 + HALF * (c + 1)] = band(rim + SPAN - cols)
    wz = band(np.arange(DEPTH)[:, None] - np.arange(DEPTH)[None, :])

    def split(a):
        a = a.astype(np.float32)
        hi = a.astype(ml_dtypes.bfloat16)
        lo = (a - hi.astype(np.float32)).astype(ml_dtypes.bfloat16)
        return hi, lo

    return split(wy) + split(wz)


def split_bf16(value):
    hi = value.astype(BF16)
    return hi, (value - hi.astype(F32)).astype(BF16)


def dot3(a, b):
    def dot(x, y):
        return jnp.dot(x, y, preferred_element_type=F32)

    return dot(a[0], b[0]) + (dot(a[1], b[0]) + dot(a[0], b[1]))


def kernel(
    vel, noise, prev, decay, stress, mean, wyh, wyl, wzh, wzl, out,
    v, s, o, hz, nz, pv, rim_out, rim_in, sm, mid, infl, psi, cols, dec,
    load_sem, rim_s, rim_r, a_s, a_r, a_l, b_s, b_r, b_l, z_s, z_r, x_s, x_r, out_sem,
):
    r, g = lax.axis_index("grp"), lax.axis_index("gx")
    xl, z, core = g // 8, lax.rem(g // 2, 4), lax.rem(g, 2)

    def by_row(values, default):
        picked = jnp.int32(default)
        for row, value in values.items():
            picked = jnp.where(r == row, value, picked)
        return picked

    count = by_row({row: len(p) for row, p in PLANES.items()}, 0)
    plane_of = [
        by_row({row: (p[j] if j < len(p) else 0) for row, p in PLANES.items()}, 0)
        for j in range(SLOTS)
    ]
    up, down = lax.rem(g + 1, COLS), lax.rem(g + COLS - 1, COLS)

    def remote(src, dst, send, recv, row, col):
        return pltpu.make_async_remote_copy(
            src_ref=src, dst_ref=dst, send_sem=send, recv_sem=recv,
            device_id=(row, col), device_id_type=MESH,
        )

    def each_slot(body):
        for j in range(SLOTS):
            pl.when(j < count)(functools.partial(body, j))

    def noise_load(j):
        return pltpu.make_async_copy(noise.at[:, plane_of[j]], nz.at[j], load_sem.at[j])

    def prev_load():
        return pltpu.make_async_copy(prev, pv, load_sem.at[SLOTS])

    def vel_load(i):
        return pltpu.make_async_copy(
            vel.at[:, pl.ds(8 * i, 8)], v.at[:, pl.ds(1 + 8 * i, 8)], load_sem.at[SLOTS + 1 + i]
        )

    each_slot(lambda j: noise_load(j).start())
    pl.when(r == 0)(lambda: prev_load().start())
    vel_load(1).start()
    pl.when(r != 0)(lambda: vel_load(0).start())

    barrier = pltpu.get_barrier_semaphore()

    def greet(row, col):
        pl.semaphore_signal(barrier, 1, device_id=(row, col), device_id_type=MESH)

    greet(r, up)
    greet(r, down)
    pl.when(r > 0)(lambda: greet(r - 1, g))
    pl.when(r < ROWS - 1)(lambda: greet(r + 1, g))

    @pl.when(count > 0)
    def _():
        for k in (1, 2, 3):
            greet(r, xl * 8 + lax.rem(z + k, 4) * 2 + core)

    @pl.when(r == 0)
    def _():
        for row in PLANES:
            for xs in range(2):
                for cs in range(2):
                    if row == 0:
                        @pl.when(jnp.logical_or(xs != xl, cs != core))
                        def _():
                            greet(row, xs * 8 + z * 2 + cs)
                    else:
                        greet(row, xs * 8 + z * 2 + cs)

    row_i = lax.broadcasted_iota(jnp.int32, (NZ, 128), 0)
    lane_i = lax.broadcasted_iota(jnp.int32, (NZ, 128), 1)

    @pl.when(r == 0)
    def _():
        mine = lane_i == row_i + NZ * g

        def column(row):
            picked = jnp.where(mine, row, 0.0)
            return jnp.broadcast_to(jnp.sum(picked, axis=1, keepdims=True), (NZ, 128))

        for c in range(3):
            cols[c] = column(decay[c : c + 1, :])
        for c in range(6):
            cols[3 + c] = column(stress[c : c + 1, :])
        cols[9] = column(mean[...])

    @pl.when(count > 0)
    def _():
        row_d = lax.broadcasted_iota(jnp.int32, (DEPTH, 128), 0)
        lane_d = lax.broadcasted_iota(jnp.int32, (DEPTH, 128), 1)
        for c in range(3):
            picked = jnp.where(row_d == lane_d, decay[c : c + 1, :], 0.0)
            dec[c] = jnp.broadcast_to(jnp.sum(picked, axis=1, keepdims=True), (DEPTH, 128))

    @pl.when(g == 0)
    def _():
        hz[0, 0] = jnp.zeros(hz.shape[2:], F32)
        hz[1, 0] = jnp.zeros(hz.shape[2:], F32)

    @pl.when(g == COLS - 1)
    def _():
        hz[0, 1] = jnp.zeros(hz.shape[2:], F32)
        hz[1, 1] = jnp.zeros(hz.shape[2:], F32)

    def clear_x(at):
        for c in range(3):
            v[c, at] = jnp.zeros((NZ, NY), F32)
            s[c, at] = jnp.zeros((NZ, NY), F32)

    pl.when(r == 0)(lambda: clear_x(0))
    pl.when(r == ROWS - 1)(lambda: clear_x(NX + 1))

    def pack(j):
        noise_load(j).wait()
        lane = lax.broadcasted_iota(jnp.int32, (DEPTH, 128), 1)
        high = jnp.zeros((DEPTH, 128), F32)
        low = jnp.zeros((DEPTH, 128), F32)
        for c in range(3):
            here = jnp.logical_and(lane >= HALF * c, lane < HALF * (c + 1))
            last = nz[j, c, :, SPAN - 128 :]
            first = nz[j, c, :, :128]
            high = jnp.where(here, pltpu.roll(last, (HALF * c + HALF) % 128, 1), high)
            low = jnp.where(here, pltpu.roll(first, HALF * c, 1) if c else first, low)
        rim_out[j, 0] = high
        rim_out[j, 1] = low

    each_slot(pack)

    waits = 2 + (r > 0).astype(jnp.int32) + (r < ROWS - 1).astype(jnp.int32)
    waits = waits + jnp.where(count > 0, 7, 0) - (r == 0).astype(jnp.int32)
    pl.semaphore_wait(barrier, waits)

    def rims(j):
        return (
            remote(rim_out.at[j, 0], rim_in.at[j, 0], rim_s.at[j, 0], rim_r.at[j, 0], r, up),
            remote(rim_out.at[j, 1], rim_in.at[j, 1], rim_s.at[j, 1], rim_r.at[j, 1], r, down),
        )

    def send_rims(j):
        for copy in rims(j):
            copy.start()

    each_slot(send_rims)

    field = (v, s)

    def z_face(stage, n, side):
        first, width = GROUPS[n]
        row = NZ - 1 if side == 0 else 0
        return remote(
            field[stage].at[:, pl.ds(1 + first, width), row],
            hz.at[stage, side, :, pl.ds(first, width), 0],
            z_s.at[stage, side, n], z_r.at[stage, side, n], r, up if side == 0 else down,
        )

    def send_z(stage, n):
        pl.when(g < COLS - 1)(lambda: z_face(stage, n, 0).start())
        pl.when(g > 0)(lambda: z_face(stage, n, 1).start())

    def recv_z(stage, n):
        pl.when(g > 0)(lambda: z_face(stage, n, 0).wait_recv())
        pl.when(g < COLS - 1)(lambda: z_face(stage, n, 1).wait_recv())

    def sent_z(stage, n):
        pl.when(g < COLS - 1)(lambda: z_face(stage, n, 0).wait_send())
        pl.when(g > 0)(lambda: z_face(stage, n, 1).wait_send())

    def x_face(stage, side):
        src, dst, row = (NX, 0, r + 1) if side == 0 else (1, NX + 1, r - 1)
        return remote(
            field[stage].at[:, src], field[stage].at[:, dst],
            x_s.at[stage, side], x_r.at[stage, side], row, g,
        )

    def send_x(stage, side):
        pl.when(r < ROWS - 1 if side == 0 else r > 0)(lambda: x_face(stage, side).start())

    def sent_x(stage, side):
        pl.when(r < ROWS - 1 if side == 0 else r > 0)(lambda: x_face(stage, side).wait_send())

    def recv_x(stage, side):
        pl.when(r > 0 if side == 0 else r < ROWS - 1)(lambda: x_face(stage, side).wait_recv())

    def a_copy(j, k):
        there = lax.rem(z + k, 4)
        return remote(
            sm.at[j, :, :, there], mid.at[j, z], a_s.at[j, k], a_r.at[j, k],
            r, xl * 8 + there * 2 + core,
        )

    def a_local(j):
        return pltpu.make_async_copy(sm.at[j, :, :, z], mid.at[j, z], a_l.at[j])

    def smooth(j):
        for copy in rims(j):
            copy.wait_recv()
        rim = jnp.concatenate([rim_in[j, 0], rim_in[j, 1]], axis=1)
        rim = split_bf16(rim)

        def one(c, carry):
            main = split_bf16(nz[j, c])
            a = tuple(jnp.concatenate([m, w], axis=1) for m, w in zip(main, rim))
            along_y = dot3(a, (wyh[c], wyl[c]))
            done = dot3((wzh[...], wzl[...]), split_bf16(along_y))
            d = dec[c][:, :1]
            done = jnp.sqrt(1.0 - d * d) * done
            sm[j, c] = done.reshape(2, 4, 2, NZ, SPAN)
            return carry

        lax.fori_loop(0, 3, one, 0)
        if j == 0:
            @pl.when(r == 0)
            def _():
                prev_load().wait()
                for c in range(3):
                    first = sm[j, c].reshape(DEPTH, SPAN) + dec[c][:, :1] * pv[c]
                    sm[j, c] = first.reshape(2, 4, 2, NZ, SPAN)
        for k in (2, 1, 3):
            a_copy(j, k).start()
        a_local(j).start()

    def b_copy(j, p, xd, cd):
        return remote(
            mid.at[j, :, :, xd, cd], infl.at[p, xl, core], b_s.at[j, xd, cd], b_r.at[p, xl, core],
            0, xd * 8 + z * 2 + cd,
        )

    def b_local(j, p):
        return pltpu.make_async_copy(mid.at[j, :, :, xl, core], infl.at[p, xl, core], b_l.at[j])

    def leaving(xd, cd):
        return jnp.logical_or(r != 0, jnp.logical_or(xl != xd, core != cd))

    def forward(j):
        for k in (1, 3, 2):
            a_copy(j, k).wait()
        a_local(j).wait()
        p = plane_of[j]
        for xd in range(2):
            for cd in range(2):
                pl.when(leaving(xd, cd))(lambda: b_copy(j, p, xd, cd).start())
        pl.when(r == 0)(lambda: b_local(j, p).start())

    def forwarded(j):
        p = plane_of[j]
        for xd in range(2):
            for cd in range(2):
                pl.when(leaving(xd, cd))(lambda: b_copy(j, p, xd, cd).wait_send())
        for copy in rims(j):
            copy.wait_send()

    def inflow(p):
        owner, j = OWNER[p]
        for xs in range(2):
            for cs in range(2):
                arrival = remote(
                    mid.at[j, :, :, 0, 0], infl.at[p, xs, cs], b_s.at[0, 0, 0], b_r.at[p, xs, cs],
                    0, xs * 8 + z * 2 + cs,
                )
                if owner == 0:
                    pl.when(jnp.logical_or(xl != xs, core != cs))(arrival.wait_recv)
                else:
                    arrival.wait_recv()
        if owner == 0:
            b_local(j, p).wait()

        def block(i, carry):
            lanes = pl.ds(pl.multiple_of(i * SPAN, SPAN), SPAN)
            at = (p, i // 8, lax.rem(i, 2), lax.rem(i // 2, 4))
            t = []
            for c in range(3):
                value = infl[at + (c,)]
                if p:
                    value = value + cols[c][:, :1] * psi[c, :, lanes]
                psi[c, :, lanes] = value
                t.append(value)
            f = [cols[3 + c][:, :1] for c in range(6)]
            v[0, p + 1, :, lanes] = cols[9][:, :1] + f[0] * t[0]
            v[1, p + 1, :, lanes] = f[1] * t[0] + f[2] * t[1]
            v[2, p + 1, :, lanes] = f[3] * t[0] + f[4] * t[1] + f[5] * t[2]
            return carry

        lax.fori_loop(0, COLS, block, 0)

    sub = lax.broadcasted_iota(jnp.int32, (NZ, WIDE), 0)
    chunks = NY // WIDE

    def section(stage, first, number):
        src = field[stage]
        half = 1.0 if stage == 0 else 0.5
        k_spread = TIME_STEP * VISCOSITY * half
        k_advect = TIME_STEP * 0.5 * half
        k_centre = half - 6.0 * k_spread

        def body(i, carry):
            x = first + i // chunks
            y = lax.rem(i, chunks)
            here = pl.ds(pl.multiple_of(y * WIDE, WIDE), WIDE)
            left = pl.ds(pl.multiple_of(lax.rem(y * WIDE + NY - 128, NY), 128), 128)
            right = pl.ds(pl.multiple_of(lax.rem(y * WIDE + WIDE, NY), 128), 128)
            centre = [src[c, x + 1, :, here] for c in range(3)]
            u = [k_advect * value for value in centre]
            to_next = [k_spread - value for value in u]
            to_prev = [k_spread + value for value in u]
            for c in range(3):
                mid_c = centre[c]
                y_prev = jnp.concatenate([src[c, x + 1, :, left], mid_c], axis=1)
                y_prev = pltpu.roll(y_prev, 1, 1)[:, 128:]
                y_next = jnp.concatenate([mid_c, src[c, x + 1, :, right]], axis=1)
                y_next = pltpu.roll(y_next, WIDE + 127, 1)[:, :WIDE]
                z_prev = jnp.where(sub == 0, hz[stage, 0, c, x, :, here], pltpu.roll(mid_c, 1, 0))
                z_next = jnp.where(
                    sub == NZ - 1, hz[stage, 1, c, x, :, here], pltpu.roll(mid_c, NZ - 1, 0)
                )
                total = k_centre * mid_c
                total = total + (to_next[0] * src[c, x + 2, :, here] + to_prev[0] * src[c, x, :, here])
                total = total + (to_next[1] * z_next + to_prev[1] * z_prev)
                total = total + (to_next[2] * y_next + to_prev[2] * y_prev)
                if stage == 0:
                    s[c, x + 1, :, here] = total
                else:
                    o[c, x, :, here] = total + 0.5 * v[c, x + 1, :, here]
            return carry

        lax.fori_loop(0, number * chunks, body, 0)

    def flush(n, first, number):
        return pltpu.make_async_copy(
            o.at[:, pl.ds(first, number)], out.at[:, pl.ds(first, number)], out_sem.at[n]
        )

    vel_load(1).wait()
    send_x(0, 0)
    send_z(0, 5)
    send_z(0, 4)

    @pl.when(r != 0)
    def _():
        vel_load(0).wait()
        x_face(0, 1).start()
        for n in range(4):
            send_z(0, n)

    each_slot(smooth)
    each_slot(forward)

    recv_z(0, 5)
    section(0, 12, 3)
    recv_z(0, 4)
    section(0, 9, 3)
    recv_x(0, 1)
    section(0, 15, 1)
    send_x(1, 0)
    send_z(1, 5)

    @pl.when(r == 0)
    def _():
        for p in range(PL):
            inflow(p)
            if p % 2 == 1:
                send_z(0, p // 2)

    recv_x(0, 0)
    recv_z(0, 0)
    section(0, 0, 1)
    send_x(1, 1)
    for n in range(4):
        if n < 3:
            recv_z(0, n + 1)
        section(0, GROUPS[n][0] + 1, 2)
        send_z(1, n)
    send_z(1, 4)

    recv_z(1, 5)
    section(1, 13, 2)
    flush(0, 13, 2).start()
    recv_z(1, 0)
    section(1, 1, 1)
    for n in range(1, 4):
        recv_z(1, n)
        section(1, GROUPS[n][0], 2)
    flush(1, 1, 7).start()
    recv_z(1, 4)
    section(1, 8, 5)
    flush(2, 8, 5).start()
    recv_x(1, 1)
    section(1, 15, 1)
    flush(3, 15, 1).start()
    recv_x(1, 0)
    section(1, 0, 1)
    flush(4, 0, 1).start()

    each_slot(forwarded)
    for stage in range(2):
        for n in range(NG):
            sent_z(stage, n)
        for side in range(2):
            sent_x(stage, side)
    flush(0, 13, 2).wait()
    flush(1, 1, 7).wait()
    flush(2, 8, 5).wait()
    flush(3, 15, 1).wait()
    flush(4, 0, 1).wait()


def local(velocity, noise, previous, decay, stress_factor, mean_profile):
    vmem = pl.BlockSpec(memory_space=pltpu.VMEM)
    hbm = pl.BlockSpec(memory_space=pl.ANY)
    dma = pltpu.SemaphoreType.DMA
    buffers = [
        (3, NX + 2, NZ, NY), (3, NX + 2, NZ, NY), (3, NX, NZ, NY), (2, 2, 3, NX, 1, NY),
        (SLOTS, 3, DEPTH, SPAN), (3, DEPTH, SPAN), (SLOTS, 2, DEPTH, 128), (SLOTS, 2, DEPTH, 128),
        (SLOTS, 3, 2, 4, 2, NZ, SPAN), (SLOTS, 4, 3, 2, 2, NZ, SPAN),
        (PL, 2, 2, 4, 3, NZ, SPAN), (3, NZ, NY), (10, NZ, 128), (3, DEPTH, 128),
    ]
    call = pl.pallas_call(
        kernel,
        out_shape=jax.ShapeDtypeStruct((3, NX, NZ, NY), F32),
        in_specs=[hbm, hbm, hbm] + [vmem] * 7,
        out_specs=hbm,
        scratch_shapes=[pltpu.VMEM(shape, F32) for shape in buffers]
        + [
            dma((SLOTS + 3,)), dma((SLOTS, 2)), dma((SLOTS, 2)), dma((SLOTS, 4)), dma((SLOTS, 4)),
            dma((SLOTS,)), dma((SLOTS, 2, 2)), dma((PL, 2, 2)), dma((SLOTS,)),
            dma((2, 2, NG)), dma((2, 2, NG)), dma((2, 2)), dma((2, 2)), dma((5,)),
        ],
        compiler_params=pltpu.CompilerParams(
            collective_id=0, has_side_effects=True, vmem_limit_bytes=58 * 2**20
        ),
        name="inflow_step",
    )
    return call(
        velocity, noise, previous, decay, stress_factor, mean_profile[None, :],
        *(jnp.asarray(w) for w in weights()),
    )


def solution(mesh):
    placed = (
        P(None, "grp", "gx", None),
        P(None, None, None, "gx"),
        P(None, None, "gx"),
        P(),
        P(),
        P(),
    )
    return jax.shard_map(
        local, mesh=mesh, in_specs=placed, out_specs=P(None, "grp", "gx", None), check_vma=False
    )
```

time: 209 us -> 86 us (0.41)
  Pallas kernels: 0 us -> 79.6 us
  waiting for transfers between devices: 72.7 us -> 0 us
  local copies, waits for them, and re-layouts: 50.9 us -> 6.2 us
  other arithmetic: 39.1 us -> 0 us
  starting transfers between devices: 32.6 us -> 0 us
  matrix products: 10.3 us -> 0 us
    pallas_call x0 -> x1, Pallas kernels: none -> 79.6 us  [local(): call(velocity, noise, previous, decay, stress_factor, mean_profile[None,...]
    ppermute x10 -> x0, waiting for transfers between devices: 37.2 us -> none  [the longest x5 22.3 us: with_halo(): after = lax.ppermute(leading, axis, down)]
    all_to_all x1 -> x0, waiting for transfers between devices: 35.5 us -> none  [to_owners(): lax.all_to_all(generated, 'gx', split_axis=2, concat_axis=3, tiled=True)]
    slice x12 -> x0, local copies, waits for them, and re-layouts: 28.3 us -> none  [the longest x4 19.6 us: tendency(): y_next = jnp.roll(centre, -1, axis=3)]
    ppermute x10 -> x0, starting transfers between devices: 26.5 us -> none  [the longest x5 19.4 us: with_halo(): after = lax.ppermute(leading, axis, down)]
    add x3 -> x0, other arithmetic: 24.7 us -> none  [the longest x1 12.9 us: local(): return 0.5 * start + 0.5 * second]
    concatenate x3 -> x0, other arithmetic: 12 us -> none  [with_halo(): array = jnp.concatenate([before, array, after], axis=dim)]
    dot_general x2 -> x0, matrix products: 10.3 us -> none  [the longest x1 7.71 us: filtered(): jnp.einsum('cpzj,jy->cpzy', widened, y_band, precision=lax.Precision.HIGH...]
  transfers between devices with their start and end apart: 11 -> 0, of which waited for: 8 -> 0; matrix products, arithmetic and copies ran while one was open for 15% -> 0% of each run, Pallas kernels for 0% -> 0%
where the time goes in v1:
time: 86 us; the launch traced here: 85.8 us
  Pallas kernels  79.6 us (93%)
  local copies, waits for them, and re-layouts  6.2 us (7%)
    pallas_call x1, Pallas kernels, local(): call(velocity, noise, previous, decay, stress_factor, mean_profile[None,...  79.6 us
    unnamed x1, local copies, waits for them, and re-layouts  6.2 us

profile of v1, /device:TPU:2, one launch (start us, length us, event | category | flops | bytes accessed | tf_op | source)
XLA Modules:
  0.0 85.8 jit_solution(12116701052500715536)
XLA Ops:
  0.0 79.6 %inflow_step.1 = f32[3,16,8,4096]{3,2,1,0:T(8,128)} custom-call(f32[3,16,8,4096]{3,2,1,0:T(8,128)} %vel.1, f32[3,8,128,256]{3,2,1,0:T(8,128)} %noise.1, f32[3,128,256]{2,1,0:T(8,128)} %prev.1, f32[3,128]{1,0:T(4,128)} %decay.1, f32[6,128]{1,0:T(8,128)} %stress.1, f32[1,128]{1,0:T(1,128)} %bitcast.1, bf16[3,512,256]{2,1,0:T(8,128)(2,1)} %constant.8.clone.wyh, ...), custom_call_target="tpu_custom_call" | custom-call | tf_op jit(solution)/shard_map/inflow_step/pallas_call | solution.py:509
  79.6 6.2 %copy.12 = f32[3,16,8,4096]{3,2,1,0:T(8,128)} copy(f32[3,16,8,4096]{3,2,1,0:T(8,128)} %inflow_step.1) | data formatting | bytes 12582912

commit v2 on v1

--- a/solution.py
+++ b/solution.py
@@ -17,15 +17,14 @@
 NX, NZ, NY = 16, 8, 4096
 SPAN = NY // COLS
 DEPTH = NZ * COLS
-WIDE = 512
 MESH = pl.DeviceIdType.MESH
 F32, BF16 = jnp.float32, jnp.bfloat16
 
-PLANES = {0: (0, 4, 5, 6), 1: (1,), 3: (2,), 4: (3, 7)}
+PLANES = {0: (0, 4, 6), 1: (1, 5), 3: (2, 7), 4: (3,)}
 SLOTS = max(len(v) for v in PLANES.values())
 OWNER = {p: (r, j) for r, v in PLANES.items() for j, p in enumerate(v)}
 
-GROUPS = ((0, 2), (2, 2), (4, 2), (6, 2), (8, 4), (12, 4))
+GROUPS = ((0, 2), (2, 2), (4, 2), (6, 2), (8, 1), (9, 3), (12, 3), (15, 1))
 NG = len(GROUPS)
 
 
@@ -41,12 +40,11 @@
 
     cols = np.arange(SPAN)[None, :]
     main = band(np.arange(SPAN)[:, None] - cols)
-    wy = np.zeros((3, SPAN + 256, SPAN))
-    for c in range(3):
-        wy[c, :SPAN] = main
-        rim = np.arange(HALF)[:, None]
-        wy[c, SPAN + HALF * c : SPAN + HALF * (c + 1)] = band(rim - HALF - cols)
-        wy[c, SPAN + 128 + HALF * c : SPAN + 128 + HALF * (c + 1)] = band(rim + SPAN - cols)
+    wy = np.zeros((SPAN + 128, SPAN))
+    wy[:SPAN] = main
+    rim = np.arange(HALF)[:, None]
+    wy[SPAN : SPAN + HALF] = band(rim - HALF - cols)
+    wy[SPAN + HALF : SPAN + 2 * HALF] = band(rim + SPAN - cols)
     wz = band(np.arange(DEPTH)[:, None] - np.arange(DEPTH)[None, :])
 
     def split(a):
@@ -55,7 +53,8 @@
         lo = (a - hi.astype(np.float32)).astype(ml_dtypes.bfloat16)
         return hi, lo
 
-    return split(wy) + split(wz)
+    zh, zl = split(wz)
+    return split(wy) + (np.concatenate([zh, zl]),)
 
 
 def split_bf16(value):
@@ -63,17 +62,14 @@
     return hi, (value - hi.astype(F32)).astype(BF16)
 
 
-def dot3(a, b):
-    def dot(x, y):
-        return jnp.dot(x, y, preferred_element_type=F32)
-
-    return dot(a[0], b[0]) + (dot(a[1], b[0]) + dot(a[0], b[1]))
+def dot(a, b):
+    return jnp.dot(a, b, preferred_element_type=F32)
 
 
 def kernel(
-    vel, noise, prev, decay, stress, mean, wyh, wyl, wzh, wzl, out,
-    v, s, o, hz, nz, pv, rim_out, rim_in, sm, mid, infl, psi, cols, dec,
-    load_sem, rim_s, rim_r, a_s, a_r, a_l, b_s, b_r, b_l, z_s, z_r, x_s, x_r, out_sem,
+    vel, noise, prev, decay, stress, mean, wyh, wyl, wz, o,
+    v, s, hz, nz, pv, rim_out, rim_in, sm, mid, infl, psi, cols, dec,
+    load_sem, rim_s, rim_r, a_s, a_r, b_s, b_r, b_l, z_s, z_r, x_s, x_r,
 ):
     r, g = lax.axis_index("grp"), lax.axis_index("gx")
     xl, z, core = g // 8, lax.rem(g // 2, 4), lax.rem(g, 2)
@@ -265,26 +261,27 @@
             r, xl * 8 + there * 2 + core,
         )
 
-    def a_local(j):
-        return pltpu.make_async_copy(sm.at[j, :, :, z], mid.at[j, z], a_l.at[j])
-
     def smooth(j):
         for copy in rims(j):
             copy.wait_recv()
-        rim = jnp.concatenate([rim_in[j, 0], rim_in[j, 1]], axis=1)
-        rim = split_bf16(rim)
-
-        def one(c, carry):
-            main = split_bf16(nz[j, c])
-            a = tuple(jnp.concatenate([m, w], axis=1) for m, w in zip(main, rim))
-            along_y = dot3(a, (wyh[c], wyl[c]))
-            done = dot3((wzh[...], wzl[...]), split_bf16(along_y))
+        lane = lax.broadcasted_iota(jnp.int32, (DEPTH, 128), 1)
+        low, high = rim_in[j, 0], rim_in[j, 1]
+        rows = []
+        for c in range(3):
+            before = pltpu.roll(low, (128 - HALF * c) % 128, 1) if c else low
+            after = pltpu.roll(high, (128 + HALF - HALF * c) % 128, 1) if c != 1 else high
+            rim = jnp.where(lane < HALF, before, jnp.where(lane < 2 * HALF, after, 0.0))
+            rows.append(jnp.concatenate([nz[j, c], rim], axis=1))
+        hi, lo = split_bf16(jnp.concatenate(rows, axis=0))
+        both = dot(jnp.concatenate([hi, lo], axis=0), wyh[...])
+        along_y = (both[: 3 * DEPTH] + both[3 * DEPTH :]) + dot(hi, wyl[...])
+        for c in range(3):
+            hi, lo = split_bf16(along_y[DEPTH * c : DEPTH * (c + 1)])
+            both = dot(wz[...], hi)
+            done = (both[:DEPTH] + both[DEPTH:]) + dot(wz[:DEPTH], lo)
             d = dec[c][:, :1]
             done = jnp.sqrt(1.0 - d * d) * done
             sm[j, c] = done.reshape(2, 4, 2, NZ, SPAN)
-            return carry
-
-        lax.fori_loop(0, 3, one, 0)
         if j == 0:
             @pl.when(r == 0)
             def _():
@@ -294,35 +291,45 @@
                     sm[j, c] = first.reshape(2, 4, 2, NZ, SPAN)
         for k in (2, 1, 3):
             a_copy(j, k).start()
-        a_local(j).start()
-
-    def b_copy(j, p, xd, cd):
+        pass_on(j, 0)
+
+    def b_copy(j, k, xd, cd):
+        here = lax.rem(z + k, 4)
+        src = mid.at[j, here, :, xd, cd] if k else sm.at[j, :, xd, z, cd]
         return remote(
-            mid.at[j, :, :, xd, cd], infl.at[p, xl, core], b_s.at[j, xd, cd], b_r.at[p, xl, core],
-            0, xd * 8 + z * 2 + cd,
-        )
-
-    def b_local(j, p):
-        return pltpu.make_async_copy(mid.at[j, :, :, xl, core], infl.at[p, xl, core], b_l.at[j])
+            src, infl.at[plane_of[j], xl, core, here], b_s.at[j, xd, cd],
+            b_r.at[plane_of[j], xl, core], 0, xd * 8 + z * 2 + cd,
+        )
+
+    def b_local(j, k):
+        here = lax.rem(z + k, 4)
+        src = mid.at[j, here, :, xl, core] if k else sm.at[j, :, xl, z, core]
+        return pltpu.make_async_copy(src, infl.at[plane_of[j], xl, core, here], b_l.at[j])
 
     def leaving(xd, cd):
         return jnp.logical_or(r != 0, jnp.logical_or(xl != xd, core != cd))
 
+    def pass_on(j, k):
+        for xd in range(2):
+            for cd in range(2):
+                pl.when(leaving(xd, cd))(lambda: b_copy(j, k, xd, cd).start())
+        pl.when(r == 0)(lambda: b_local(j, k).start())
+
     def forward(j):
         for k in (1, 3, 2):
-            a_copy(j, k).wait()
-        a_local(j).wait()
-        p = plane_of[j]
+            a_copy(j, (4 - k) % 4).wait_recv()
+            pass_on(j, k)
+
+    def forwarded(j):
         for xd in range(2):
             for cd in range(2):
-                pl.when(leaving(xd, cd))(lambda: b_copy(j, p, xd, cd).start())
-        pl.when(r == 0)(lambda: b_local(j, p).start())
-
-    def forwarded(j):
-        p = plane_of[j]
-        for xd in range(2):
-            for cd in range(2):
-                pl.when(leaving(xd, cd))(lambda: b_copy(j, p, xd, cd).wait_send())
+                whole = remote(
+                    mid.at[j, :, :, 0, 0], infl.at[0, 0, 0], b_s.at[j, xd, cd], b_r.at[0, 0, 0],
+                    0, xd * 8 + z * 2 + cd,
+                )
+                pl.when(leaving(xd, cd))(whole.wait_send)
+        for k in (1, 2, 3):
+            a_copy(j, k).wait_send()
         for copy in rims(j):
             copy.wait_send()
 
@@ -339,7 +346,7 @@
                 else:
                     arrival.wait_recv()
         if owner == 0:
-            b_local(j, p).wait()
+            pltpu.make_async_copy(mid.at[j, :, :, 0, 0], infl.at[p, 0, 0], b_l.at[j]).wait()
 
         def block(i, carry):
             lanes = pl.ds(pl.multiple_of(i * SPAN, SPAN), SPAN)
@@ -357,10 +364,9 @@
             v[2, p + 1, :, lanes] = f[3] * t[0] + f[4] * t[1] + f[5] * t[2]
             return carry
 
-        lax.fori_loop(0, COLS, block, 0)
-
-    sub = lax.broadcasted_iota(jnp.int32, (NZ, WIDE), 0)
-    chunks = NY // WIDE
+        lax.fori_loop(0, COLS, block, 0, unroll=8)
+
+    sub = lax.broadcasted_iota(jnp.int32, (NZ, NY), 0)
 
     def section(stage, first, number):
         src = field[stage]
@@ -370,102 +376,108 @@
         k_centre = half - 6.0 * k_spread
 
         def body(i, carry):
-            x = first + i // chunks
-            y = lax.rem(i, chunks)
-            here = pl.ds(pl.multiple_of(y * WIDE, WIDE), WIDE)
-            left = pl.ds(pl.multiple_of(lax.rem(y * WIDE + NY - 128, NY), 128), 128)
-            right = pl.ds(pl.multiple_of(lax.rem(y * WIDE + WIDE, NY), 128), 128)
-            centre = [src[c, x + 1, :, here] for c in range(3)]
+            x = first + i
+            centre = [src[c, x + 1] for c in range(3)]
             u = [k_advect * value for value in centre]
             to_next = [k_spread - value for value in u]
             to_prev = [k_spread + value for value in u]
             for c in range(3):
                 mid_c = centre[c]
-                y_prev = jnp.concatenate([src[c, x + 1, :, left], mid_c], axis=1)
-                y_prev = pltpu.roll(y_prev, 1, 1)[:, 128:]
-                y_next = jnp.concatenate([mid_c, src[c, x + 1, :, right]], axis=1)
-                y_next = pltpu.roll(y_next, WIDE + 127, 1)[:, :WIDE]
-                z_prev = jnp.where(sub == 0, hz[stage, 0, c, x, :, here], pltpu.roll(mid_c, 1, 0))
-                z_next = jnp.where(
-                    sub == NZ - 1, hz[stage, 1, c, x, :, here], pltpu.roll(mid_c, NZ - 1, 0)
-                )
+                y_prev, y_next = pltpu.roll(mid_c, 1, 1), pltpu.roll(mid_c, NY - 1, 1)
+                z_prev = jnp.where(sub == 0, hz[stage, 0, c, x], pltpu.roll(mid_c, 1, 0))
+                z_next = jnp.where(sub == NZ - 1, hz[stage, 1, c, x], pltpu.roll(mid_c, NZ - 1, 0))
                 total = k_centre * mid_c
-                total = total + (to_next[0] * src[c, x + 2, :, here] + to_prev[0] * src[c, x, :, here])
+                total = total + (to_next[0] * src[c, x + 2] + to_prev[0] * src[c, x])
                 total = total + (to_next[1] * z_next + to_prev[1] * z_prev)
                 total = total + (to_next[2] * y_next + to_prev[2] * y_prev)
                 if stage == 0:
-                    s[c, x + 1, :, here] = total
+                    s[c, x + 1] = total
                 else:
-                    o[c, x, :, here] = total + 0.5 * v[c, x + 1, :, here]
+                    o[c, x] = total + 0.5 * v[c, x + 1]
             return carry
 
-        lax.fori_loop(0, number * chunks, body, 0)
-
-    def flush(n, first, number):
-        return pltpu.make_async_copy(
-            o.at[:, pl.ds(first, number)], out.at[:, pl.ds(first, number)], out_sem.at[n]
-        )
+        lax.fori_loop(0, number, body, 0)
+
+    def start_faces():
+        for n in range(4):
+            send_z(0, n)
+
+    @pl.when(r != 0)
+    def _():
+        vel_load(0).wait()
+        x_face(0, 1).start()
 
     vel_load(1).wait()
     send_x(0, 0)
-    send_z(0, 5)
-    send_z(0, 4)
-
-    @pl.when(r != 0)
-    def _():
-        vel_load(0).wait()
-        x_face(0, 1).start()
-        for n in range(4):
-            send_z(0, n)
-
+    for n in (6, 5, 4, 7):
+        send_z(0, n)
+    pl.when(count == 0)(start_faces)
     each_slot(smooth)
+    pl.when(jnp.logical_and(count > 0, r != 0))(start_faces)
     each_slot(forward)
 
+    recv_z(0, 6)
+    section(0, 12, 3)
+    send_z(1, 6)
     recv_z(0, 5)
-    section(0, 12, 3)
-    recv_z(0, 4)
     section(0, 9, 3)
+    send_z(1, 5)
+    recv_z(0, 7)
     recv_x(0, 1)
     section(0, 15, 1)
     send_x(1, 0)
-    send_z(1, 5)
-
-    @pl.when(r == 0)
-    def _():
-        for p in range(PL):
-            inflow(p)
-            if p % 2 == 1:
-                send_z(0, p // 2)
-
+    send_z(1, 7)
+
+    def arrive(*planes):
+        @pl.when(r == 0)
+        def _():
+            for p in planes:
+                inflow(p)
+                if p % 2 == 1:
+                    send_z(0, p // 2)
+
+    def upper():
+        recv_z(1, 6)
+        recv_z(1, 5)
+        section(1, 10, 4)
+        recv_z(1, 7)
+        section(1, 14, 1)
+
+    pl.when(r == 0)(upper)
+    arrive(0, 1, 2, 3)
     recv_x(0, 0)
     recv_z(0, 0)
-    section(0, 0, 1)
+    section(0, 0, 2)
     send_x(1, 1)
-    for n in range(4):
-        if n < 3:
-            recv_z(0, n + 1)
-        section(0, GROUPS[n][0] + 1, 2)
-        send_z(1, n)
+    recv_z(0, 1)
+    section(0, 2, 1)
+    send_z(1, 0)
+    arrive(4, 5)
+    section(0, 3, 1)
+    send_z(1, 1)
+    arrive(6, 7)
+    recv_z(0, 2)
+    section(0, 4, 2)
+    send_z(1, 2)
+    recv_z(0, 3)
+    recv_z(0, 4)
+    section(0, 6, 3)
+    send_z(1, 3)
     send_z(1, 4)
 
-    recv_z(1, 5)
-    section(1, 13, 2)
-    flush(0, 13, 2).start()
+    pl.when(r != 0)(upper)
     recv_z(1, 0)
     section(1, 1, 1)
-    for n in range(1, 4):
-        recv_z(1, n)
-        section(1, GROUPS[n][0], 2)
-    flush(1, 1, 7).start()
-    recv_z(1, 4)
-    section(1, 8, 5)
-    flush(2, 8, 5).start()
+    recv_z(1, 1)
+    recv_z(1, 2)
+    section(1, 2, 3)
+    recv_x(1, 0)
+    section(1, 0, 1)
     recv_x(1, 1)
     section(1, 15, 1)
-    flush(3, 15, 1).start()
-    recv_x(1, 0)
-    section(1, 0, 1)
-    flush(4, 0, 1).start()
+    recv_z(1, 3)
+    recv_z(1, 4)
+    section(1, 5, 5)
 
     each_slot(forwarded)
     for stage in range(2):
@@ -473,11 +485,18 @@
             sent_z(stage, n)
         for side in range(2):
             sent_x(stage, side)
-    flush(0, 13, 2).wait()
-    flush(1, 1, 7).wait()
-    flush(2, 8, 5).wait()
-    flush(3, 15, 1).wait()
-    flush(4, 0, 1).wait()
+
+
+def store(src, dst, sem):
+    copies = []
+    for c in range(3):
+        for i in range(4):
+            part = pl.ds(4 * i, 4)
+            copies.append(pltpu.make_async_copy(src.at[c, part], dst.at[c, part], sem.at[c, i]))
+    for copy in copies:
+        copy.start()
+    for copy in copies:
+        copy.wait()
 
 
 def local(velocity, noise, previous, decay, stress_factor, mean_profile):
@@ -485,31 +504,40 @@
     hbm = pl.BlockSpec(memory_space=pl.ANY)
     dma = pltpu.SemaphoreType.DMA
     buffers = [
-        (3, NX + 2, NZ, NY), (3, NX + 2, NZ, NY), (3, NX, NZ, NY), (2, 2, 3, NX, 1, NY),
+        (3, NX + 2, NZ, NY), (3, NX + 2, NZ, NY), (2, 2, 3, NX, 1, NY),
         (SLOTS, 3, DEPTH, SPAN), (3, DEPTH, SPAN), (SLOTS, 2, DEPTH, 128), (SLOTS, 2, DEPTH, 128),
         (SLOTS, 3, 2, 4, 2, NZ, SPAN), (SLOTS, 4, 3, 2, 2, NZ, SPAN),
         (PL, 2, 2, 4, 3, NZ, SPAN), (3, NZ, NY), (10, NZ, 128), (3, DEPTH, 128),
     ]
     call = pl.pallas_call(
         kernel,
-        out_shape=jax.ShapeDtypeStruct((3, NX, NZ, NY), F32),
-        in_specs=[hbm, hbm, hbm] + [vmem] * 7,
-        out_specs=hbm,
+        out_shape=pltpu.VMEM((3, NX, NZ, NY), F32),
+        in_specs=[hbm, hbm, hbm] + [vmem] * 6,
+        out_specs=vmem,
         scratch_shapes=[pltpu.VMEM(shape, F32) for shape in buffers]
         + [
             dma((SLOTS + 3,)), dma((SLOTS, 2)), dma((SLOTS, 2)), dma((SLOTS, 4)), dma((SLOTS, 4)),
-            dma((SLOTS,)), dma((SLOTS, 2, 2)), dma((PL, 2, 2)), dma((SLOTS,)),
-            dma((2, 2, NG)), dma((2, 2, NG)), dma((2, 2)), dma((2, 2)), dma((5,)),
+            dma((SLOTS, 2, 2)), dma((PL, 2, 2)), dma((SLOTS,)),
+            dma((2, 2, NG)), dma((2, 2, NG)), dma((2, 2)), dma((2, 2)),
         ],
         compiler_params=pltpu.CompilerParams(
-            collective_id=0, has_side_effects=True, vmem_limit_bytes=58 * 2**20
+            collective_id=0, has_side_effects=True, vmem_limit_bytes=48 * 2**20
         ),
         name="inflow_step",
     )
-    return call(
+    done = call(
         velocity, noise, previous, decay, stress_factor, mean_profile[None, :],
         *(jnp.asarray(w) for w in weights()),
     )
+    return pl.pallas_call(
+        store,
+        out_shape=jax.ShapeDtypeStruct(done.shape, F32),
+        in_specs=[vmem],
+        out_specs=hbm,
+        scratch_shapes=[dma((3, 4))],
+        compiler_params=pltpu.CompilerParams(vmem_limit_bytes=2**20),
+        name="store",
+    )(done)
 
 
 def solution(mesh):

time: 86 us -> 63.2 us (0.73)
  Pallas kernels: 79.6 us -> 62.6 us
  local copies, waits for them, and re-layouts: 6.2 us -> 0 us
    pallas_call x1, Pallas kernels: 79.6 us -> 59.9 us  [local(): call(velocity, noise, previous, decay, stress_factor, mean_profile[None,...]
    unnamed x1 -> x0, local copies, waits for them, and re-layouts: 6.2 us -> none
    pallas_call x0 -> x1, Pallas kernels: none -> 2.75 us  [local(): pl.pallas_call(store, out_shape=jax.ShapeDtypeStruct(done.shape, F32), in...]
where the time goes in v2:
time: 63.2 us; the launch traced here: 62.8 us
  Pallas kernels  62.6 us (99%)
    pallas_call x1, Pallas kernels, local(): call(velocity, noise, previous, decay, stress_factor, mean_profile[None,...  59.9 us
    pallas_call x1, Pallas kernels, local(): pl.pallas_call(store, out_shape=jax.ShapeDtypeStruct(done.shape, F32), in...  2.75 us

profile of v2, /device:TPU:2, one launch (start us, length us, event | category | flops | bytes accessed | tf_op | source)
XLA Modules:
  0.0 62.8 jit_solution(9358883509603946036)
XLA Ops:
  0.0 59.9 %inflow_step.1.src = f32[3,16,8,4096]{3,2,1,0:T(8,128)S(1)} custom-call(f32[3,16,8,4096]{3,2,1,0:T(8,128)} %vel.1, f32[3,8,128,256]{3,2,1,0:T(8,128)} %noise.1, f32[3,128,256]{2,1,0:T(8,128)} %prev.1, f32[3,128]{1,0:T(4,128)} %decay.1, f32[6,128]{1,0:T(8,128)} %stress.1, f32[1,128]{1,0:T(1,128)} %bitcast.1, bf16[384,256]{1,0:T(8,128)(2,1)} %constant.6.clone.wyh, ...), custom_call_target="tpu_custom_call" | custom-call | tf_op jit(solution)/shard_map/inflow_step/pallas_call | solution.py:528
  59.9 2.8 %store.1 = f32[3,16,8,4096]{3,2,1,0:T(8,128)} custom-call(f32[3,16,8,4096]{3,2,1,0:T(8,128)S(1)} %inflow_step.1.src), custom_call_target="tpu_custom_call" | custom-call | tf_op jit(solution)/shard_map/store/pallas_call | solution.py:532

commit v3 on v2

--- a/solution.py
+++ b/solution.py
@@ -20,9 +20,10 @@
 MESH = pl.DeviceIdType.MESH
 F32, BF16 = jnp.float32, jnp.bfloat16
 
-PLANES = {0: (0, 4, 6), 1: (1, 5), 3: (2, 7), 4: (3,)}
+PAIR = 4
+PLANES = {0: (0, 1, 4, 6), PAIR: (0, 1, 4, 6), 1: (3, 7), 3: (2, 5)}
 SLOTS = max(len(v) for v in PLANES.values())
-OWNER = {p: (r, j) for r, v in PLANES.items() for j, p in enumerate(v)}
+OWNER = {p: (r, j) for r, v in PLANES.items() if r != PAIR for j, p in enumerate(v)}
 
 GROUPS = ((0, 2), (2, 2), (4, 2), (6, 2), (8, 1), (9, 3), (12, 3), (15, 1))
 NG = len(GROUPS)
@@ -109,7 +110,8 @@
         )
 
     each_slot(lambda j: noise_load(j).start())
-    pl.when(r == 0)(lambda: prev_load().start())
+    first_plane = jnp.logical_or(r == 0, r == PAIR)
+    pl.when(first_plane)(lambda: prev_load().start())
     vel_load(1).start()
     pl.when(r != 0)(lambda: vel_load(0).start())
 
@@ -130,15 +132,15 @@
 
     @pl.when(r == 0)
     def _():
-        for row in PLANES:
-            for xs in range(2):
-                for cs in range(2):
-                    if row == 0:
-                        @pl.when(jnp.logical_or(xs != xl, cs != core))
-                        def _():
-                            greet(row, xs * 8 + z * 2 + cs)
-                    else:
-                        greet(row, xs * 8 + z * 2 + cs)
+        for cs in range(2):
+            for row in PLANES:
+                if row == 0:
+                    pl.when(core != cs)(lambda: greet(row, xl * 8 + z * 2 + cs))
+                elif row == PAIR:
+                    greet(row, (1 - xl) * 8 + z * 2 + cs)
+                else:
+                    greet(row, z * 2 + cs)
+                    greet(row, 8 + z * 2 + cs)
 
     row_i = lax.broadcasted_iota(jnp.int32, (NZ, 128), 0)
     lane_i = lax.broadcasted_iota(jnp.int32, (NZ, 128), 1)
@@ -200,7 +202,7 @@
     each_slot(pack)
 
     waits = 2 + (r > 0).astype(jnp.int32) + (r < ROWS - 1).astype(jnp.int32)
-    waits = waits + jnp.where(count > 0, 7, 0) - (r == 0).astype(jnp.int32)
+    waits = waits + by_row({0: 4, PAIR: 5, 1: 7, 3: 7}, 0)
     pl.semaphore_wait(barrier, waits)
 
     def rims(j):
@@ -254,10 +256,15 @@
     def recv_x(stage, side):
         pl.when(r > 0 if side == 0 else r < ROWS - 1)(lambda: x_face(stage, side).wait_recv())
 
-    def a_copy(j, k):
+    def for_side(xd, body):
+        across = xl != xd
+        used = jnp.where(r == 0, jnp.logical_not(across), jnp.where(r == PAIR, across, True))
+        pl.when(used)(body)
+
+    def a_copy(j, k, xd):
         there = lax.rem(z + k, 4)
         return remote(
-            sm.at[j, :, :, there], mid.at[j, z], a_s.at[j, k], a_r.at[j, k],
+            sm.at[j, :, xd, there], mid.at[j, xd, z], a_s.at[j, k, xd], a_r.at[j, k, xd],
             r, xl * 8 + there * 2 + core,
         )
 
@@ -283,19 +290,20 @@
             done = jnp.sqrt(1.0 - d * d) * done
             sm[j, c] = done.reshape(2, 4, 2, NZ, SPAN)
         if j == 0:
-            @pl.when(r == 0)
+            @pl.when(first_plane)
             def _():
                 prev_load().wait()
                 for c in range(3):
                     first = sm[j, c].reshape(DEPTH, SPAN) + dec[c][:, :1] * pv[c]
                     sm[j, c] = first.reshape(2, 4, 2, NZ, SPAN)
         for k in (2, 1, 3):
-            a_copy(j, k).start()
+            for xd in range(2):
+                for_side(xd, lambda: a_copy(j, k, xd).start())
         pass_on(j, 0)
 
     def b_copy(j, k, xd, cd):
         here = lax.rem(z + k, 4)
-        src = mid.at[j, here, :, xd, cd] if k else sm.at[j, :, xd, z, cd]
+        src = mid.at[j, xd, here, :, cd] if k else sm.at[j, :, xd, z, cd]
         return remote(
             src, infl.at[plane_of[j], xl, core, here], b_s.at[j, xd, cd],
             b_r.at[plane_of[j], xl, core], 0, xd * 8 + z * 2 + cd,
@@ -303,33 +311,38 @@
 
     def b_local(j, k):
         here = lax.rem(z + k, 4)
-        src = mid.at[j, here, :, xl, core] if k else sm.at[j, :, xl, z, core]
+        src = mid.at[j, xl, here, :, core] if k else sm.at[j, :, xl, z, core]
         return pltpu.make_async_copy(src, infl.at[plane_of[j], xl, core, here], b_l.at[j])
 
-    def leaving(xd, cd):
-        return jnp.logical_or(r != 0, jnp.logical_or(xl != xd, core != cd))
+    def leaving(cd):
+        return jnp.logical_or(r != 0, core != cd)
 
     def pass_on(j, k):
         for xd in range(2):
-            for cd in range(2):
-                pl.when(leaving(xd, cd))(lambda: b_copy(j, k, xd, cd).start())
+            @functools.partial(for_side, xd)
+            def _():
+                for cd in range(2):
+                    pl.when(leaving(cd))(lambda: b_copy(j, k, xd, cd).start())
         pl.when(r == 0)(lambda: b_local(j, k).start())
 
     def forward(j):
         for k in (1, 3, 2):
-            a_copy(j, (4 - k) % 4).wait_recv()
+            for xd in range(2):
+                for_side(xd, lambda: a_copy(j, (4 - k) % 4, xd).wait_recv())
             pass_on(j, k)
 
     def forwarded(j):
         for xd in range(2):
-            for cd in range(2):
-                whole = remote(
-                    mid.at[j, :, :, 0, 0], infl.at[0, 0, 0], b_s.at[j, xd, cd], b_r.at[0, 0, 0],
-                    0, xd * 8 + z * 2 + cd,
-                )
-                pl.when(leaving(xd, cd))(whole.wait_send)
-        for k in (1, 2, 3):
-            a_copy(j, k).wait_send()
+            @functools.partial(for_side, xd)
+            def _():
+                for cd in range(2):
+                    whole = remote(
+                        mid.at[j, 0, :, :, 0], infl.at[0, 0, 0], b_s.at[j, xd, cd],
+                        b_r.at[0, 0, 0], 0, xd * 8 + z * 2 + cd,
+                    )
+                    pl.when(leaving(cd))(whole.wait_send)
+                for k in (1, 2, 3):
+                    a_copy(j, k, xd).wait_send()
         for copy in rims(j):
             copy.wait_send()
 
@@ -338,7 +351,7 @@
         for xs in range(2):
             for cs in range(2):
                 arrival = remote(
-                    mid.at[j, :, :, 0, 0], infl.at[p, xs, cs], b_s.at[0, 0, 0], b_r.at[p, xs, cs],
+                    mid.at[j, 0, :, :, 0], infl.at[p, xs, cs], b_s.at[0, 0, 0], b_r.at[p, xs, cs],
                     0, xs * 8 + z * 2 + cs,
                 )
                 if owner == 0:
@@ -346,7 +359,7 @@
                 else:
                     arrival.wait_recv()
         if owner == 0:
-            pltpu.make_async_copy(mid.at[j, :, :, 0, 0], infl.at[p, 0, 0], b_l.at[j]).wait()
+            pltpu.make_async_copy(mid.at[j, 0, :, :, 0], infl.at[p, 0, 0], b_l.at[j]).wait()
 
         def block(i, carry):
             lanes = pl.ds(pl.multiple_of(i * SPAN, SPAN), SPAN)
@@ -448,6 +461,7 @@
     recv_x(0, 0)
     recv_z(0, 0)
     section(0, 0, 2)
+    pl.when(r != 0)(lambda: each_slot(forwarded))
     send_x(1, 1)
     recv_z(0, 1)
     section(0, 2, 1)
@@ -479,7 +493,7 @@
     recv_z(1, 4)
     section(1, 5, 5)
 
-    each_slot(forwarded)
+    pl.when(r == 0)(lambda: each_slot(forwarded))
     for stage in range(2):
         for n in range(NG):
             sent_z(stage, n)
@@ -506,7 +520,7 @@
     buffers = [
         (3, NX + 2, NZ, NY), (3, NX + 2, NZ, NY), (2, 2, 3, NX, 1, NY),
         (SLOTS, 3, DEPTH, SPAN), (3, DEPTH, SPAN), (SLOTS, 2, DEPTH, 128), (SLOTS, 2, DEPTH, 128),
-        (SLOTS, 3, 2, 4, 2, NZ, SPAN), (SLOTS, 4, 3, 2, 2, NZ, SPAN),
+        (SLOTS, 3, 2, 4, 2, NZ, SPAN), (SLOTS, 2, 4, 3, 2, NZ, SPAN),
         (PL, 2, 2, 4, 3, NZ, SPAN), (3, NZ, NY), (10, NZ, 128), (3, DEPTH, 128),
     ]
     call = pl.pallas_call(
@@ -516,7 +530,7 @@
         out_specs=vmem,
         scratch_shapes=[pltpu.VMEM(shape, F32) for shape in buffers]
         + [
-            dma((SLOTS + 3,)), dma((SLOTS, 2)), dma((SLOTS, 2)), dma((SLOTS, 4)), dma((SLOTS, 4)),
+            dma((SLOTS + 3,)), dma((SLOTS, 2)), dma((SLOTS, 2)), dma((SLOTS, 4, 2)), dma((SLOTS, 4, 2)),
             dma((SLOTS, 2, 2)), dma((PL, 2, 2)), dma((SLOTS,)),
             dma((2, 2, NG)), dma((2, 2, NG)), dma((2, 2)), dma((2, 2)),
         ],

time: 63.2 us -> 61.6 us (0.975)
  the two profiles are of different devices: /device:TPU:2 before, /device:TPU:101 now
where the time goes in v3:
time: 61.6 us; the launch traced here: 61.4 us
  Pallas kernels  61.3 us (100%)
    pallas_call x1, Pallas kernels, local(): call(velocity, noise, previous, decay, stress_factor, mean_profile[None,...  58.5 us
    pallas_call x1, Pallas kernels, local(): pl.pallas_call(store, out_shape=jax.ShapeDtypeStruct(done.shape, F32), in...  2.75 us

profile of v3, /device:TPU:101, one launch (start us, length us, event | category | flops | bytes accessed | tf_op | source)
XLA Modules:
  0.0 61.4 jit_solution(2582421303685515136)
XLA Ops:
  0.0 58.5 %inflow_step.1.src = f32[3,16,8,4096]{3,2,1,0:T(8,128)S(1)} custom-call(f32[3,16,8,4096]{3,2,1,0:T(8,128)} %vel.1, f32[3,8,128,256]{3,2,1,0:T(8,128)} %noise.1, f32[3,128,256]{2,1,0:T(8,128)} %prev.1, f32[3,128]{1,0:T(4,128)} %decay.1, f32[6,128]{1,0:T(8,128)} %stress.1, f32[1,128]{1,0:T(1,128)} %bitcast.1, bf16[384,256]{1,0:T(8,128)(2,1)} %constant.6.clone.wyh, ...), custom_call_target="tpu_custom_call" | custom-call | tf_op jit(solution)/shard_map/inflow_step/pallas_call | solution.py:542
  58.5 2.8 %store.1 = f32[3,16,8,4096]{3,2,1,0:T(8,128)} custom-call(f32[3,16,8,4096]{3,2,1,0:T(8,128)S(1)} %inflow_step.1.src), custom_call_target="tpu_custom_call" | custom-call | tf_op jit(solution)/shard_map/store/pallas_call | solution.py:546
